TPU v7x, 256 devices: a whole 4x4x8 slice. The times are simulated.
256 devices in a mesh: dp: 16 (over y, x_hi, core), tensor: 16 (over z, x_lo).
Axes of the slice: x: 4 (x_hi: 2, x_lo: 2; x = x_hi * 2 + x_lo), y: 4, z: 8, core: 2. Of those that a mesh axis runs over, the one named last changes fastest.
Arguments:
- hidden_in: bfloat16 [4096, 4096], P('dp'), may hold values from -6 to 6
- attn_gain: float32 [4096], replicated, may hold values from 0.5 to 1.5
- qkv_weight: bfloat16 [3, 4096, 4096], P(None, 'dp', 'tensor'), may hold values from -0.09375 to 0.09375
- mix_weight: bfloat16 [4096, 4096], P('tensor', 'dp'), may hold values from -0.09375 to 0.09375
- out_gain: float32 [4096], replicated, may hold values from 0.5 to 1.5
- depth_in_weight: bfloat16 [4096, 1024], P('tensor'), may hold values from -0.09375 to 0.09375
- text_table: bfloat16 [16000, 1024], P('tensor'), may hold values from -6 to 6
- code_tables: bfloat16 [7, 2048, 1024], P(None, 'tensor'), may hold values from -6 to 6
- depth_gain: float32 [1024], replicated, may hold values from 0.5 to 1.5
- depth_qkv: bfloat16 [3, 1024, 1024], P(None, 'dp'), may hold values from -0.1875 to 0.1875
- depth_mix: bfloat16 [1024, 1024], replicated, may hold values from -0.1875 to 0.1875
- final_gain: float32 [1024], replicated, may hold values from 0.5 to 1.5
- heads_weight: bfloat16 [8, 1024, 2048], P(None, None, 'tensor'), may hold values from -0.59765625 to 0.59765625
- text_ids: int32 [4096], P('dp'), may hold values from 0 to 15999
- codes: int32 [4096, 8], P('dp'), may hold values from 0 to 2047
Outputs:
- token_loss: float32 [4096, 8], P(('dp', 'tensor'))
All inputs are finite; a program needn't handle non-finite values.
Results may differ from a plain program's by a relative error of at most 0.005.
Values may be sent and summed in bfloat16 or wider, within the bound.
A program may use at most 128 MiB of HBM per device.

v0:
```python
import math
import jax
import jax.numpy as jnp
from jax import lax
from jax.sharding import PartitionSpec as P

D = 4096
HEAD_DIM = 128
FRAMES = 256
DD = 1024
DHEADS = 16
DHEAD_DIM = 64
CODEBOOKS = 8
epsilon = 1e-05


def rms_factor(values):
    return lax.rsqrt(jnp.mean(values * values, axis=-1, keepdims=True) + epsilon)


def rotate_halves(tensor, positions):
    half_dim = tensor.shape[-1] // 2
    frequency = jnp.exp(jnp.arange(half_dim, dtype=jnp.float32) * (-math.log(10000.0) / half_dim))
    angles = positions[:, None] * frequency[None, :]
    cosine = jnp.cos(angles)[:, None, :]
    sine_part = jnp.sin(angles)[:, None, :]
    first_half = tensor[..., :half_dim]
    second_half = tensor[..., half_dim:]
    return jnp.concatenate(
        [
            first_half * cosine - second_half * sine_part,
            second_half * cosine + first_half * sine_part,
        ],
        axis=-1,
    )


def temporal_mix(normed, qkv_cols):
    row_count = normed.shape[0]
    col_width = qkv_cols.shape[2]
    seq_count = row_count // FRAMES
    head_count = col_width // HEAD_DIM
    projected = jnp.einsum("rd,idw->irw", normed, qkv_cols, preferred_element_type=jnp.float32)
    projected = projected.reshape(3, seq_count, FRAMES, head_count, HEAD_DIM)
    positions = jnp.arange(FRAMES, dtype=jnp.float32)
    queries = rotate_halves(projected[0], positions).astype(jnp.bfloat16)
    keys_rot = rotate_halves(projected[1], positions).astype(jnp.bfloat16)
    values_all = projected[2].astype(jnp.bfloat16)
    scores = jnp.einsum(
        "sqhd,skhd->shqk", queries, keys_rot, preferred_element_type=jnp.float32
    ) * HEAD_DIM ** (-0.5)
    order = jnp.arange(FRAMES)
    causal = order[:, None] >= order[None, :]
    exp_scores = jnp.where(causal, jnp.exp(jnp.where(causal, scores, 0.0)), 0.0)
    weights = (exp_scores / jnp.sum(exp_scores, axis=-1, keepdims=True)).astype(jnp.bfloat16)
    attended = jnp.einsum(
        "shqk,skhd->sqhd", weights, values_all, preferred_element_type=jnp.float32
    )
    return attended.astype(jnp.bfloat16).reshape(row_count, col_width)


def depth_mixer(projected, mix_weight):
    row_count = projected.shape[1]
    split = projected.reshape(3, row_count, CODEBOOKS, DHEADS, DHEAD_DIM)
    scores = jnp.einsum(
        "rqhd,rkhd->rhqk", split[0], split[1], preferred_element_type=jnp.float32
    ) * DHEAD_DIM ** (-0.5)
    order = jnp.arange(CODEBOOKS)
    causal = order[:, None] >= order[None, :]
    exp_scores = jnp.where(causal, jnp.exp(jnp.where(causal, scores, 0.0)), 0.0)
    weights = (exp_scores / jnp.sum(exp_scores, axis=-1, keepdims=True)).astype(jnp.bfloat16)
    attended = jnp.einsum("rhqk,rkhd->rqhd", weights, split[2], preferred_element_type=jnp.float32)
    attended = attended.astype(jnp.bfloat16).reshape(row_count, CODEBOOKS, DD)
    return jnp.einsum("rcd,de->rce", attended, mix_weight, preferred_element_type=jnp.float32)


def local_embeds(text_table, code_tables, text_ids, codes, rank_tensor):
    text_count = text_table.shape[0]
    text_local = text_ids - rank_tensor * text_count
    text_owned = (text_local >= 0) & (text_local < text_count)
    text_found = jnp.take(text_table, jnp.clip(text_local, 0, text_count - 1), axis=0)
    text_part = jnp.where(text_owned[:, None], text_found.astype(jnp.float32), 0.0)
    code_count = code_tables.shape[1]
    code_local = codes[:, : CODEBOOKS - 1] - rank_tensor * code_count
    code_owned = (code_local >= 0) & (code_local < code_count)
    books = jnp.arange(CODEBOOKS - 1, dtype=jnp.int32)[None, :]
    code_found = code_tables[books, jnp.clip(code_local, 0, code_count - 1)]
    code_part = jnp.where(code_owned[:, :, None], code_found.astype(jnp.float32), 0.0)
    return jnp.concatenate([text_part[:, None, :], code_part], axis=1)


def arrive_embeds(embeds):
    return lax.psum_scatter(
        embeds.astype(jnp.bfloat16), "tensor", scatter_dimension=0, tiled=True
    ).astype(jnp.float32)


def shards(
    hidden_in,
    attn_gain,
    qkv_weight,
    mix_weight,
    out_gain,
    depth_in_weight,
    text_table,
    code_tables,
    depth_gain,
    depth_qkv,
    depth_mix,
    final_gain,
    heads_weight,
    text_ids,
    codes,
):
    rank_tensor = lax.axis_index("tensor")
    group_size = lax.axis_size("tensor")
    local_rows = hidden_in.shape[0]
    own_rows = local_rows // group_size
    own_start = rank_tensor * own_rows
    qkv_full, mix_full, depth_full = (
        lax.all_gather(qkv_weight, "dp", axis=1, tiled=True),
        lax.all_gather(mix_weight, "dp", axis=1, tiled=True),
        lax.all_gather(depth_qkv, "dp", axis=1, tiled=True),
    )
    hidden_f = hidden_in.astype(jnp.float32)
    normed = (hidden_f * rms_factor(hidden_f) * attn_gain).astype(jnp.bfloat16)
    attended = temporal_mix(normed, qkv_full)
    partial_mix = jnp.dot(attended, mix_full, preferred_element_type=jnp.float32)
    embeds = local_embeds(text_table, code_tables, text_ids, codes, rank_tensor)
    embed_rows = arrive_embeds(embeds)
    feat_width = depth_in_weight.shape[0]
    feat_start = rank_tensor * feat_width
    summed_cols = lax.psum_scatter(
        partial_mix.astype(jnp.bfloat16), "tensor", scatter_dimension=1, tiled=True
    ).astype(jnp.float32)
    resid_cols = summed_cols + lax.dynamic_slice_in_dim(hidden_f, feat_start, feat_width, 1)
    square_part = jnp.sum(resid_cols * resid_cols, axis=1)
    gain_cols = lax.dynamic_slice_in_dim(out_gain, feat_start, feat_width, 0)
    scaled_cols = (resid_cols * gain_cols).astype(jnp.bfloat16)
    context_part = jnp.dot(scaled_cols, depth_in_weight, preferred_element_type=jnp.float32)
    context_sum, square_sum = (
        lax.psum_scatter(
            context_part.astype(jnp.bfloat16), "tensor", scatter_dimension=0, tiled=True
        ).astype(jnp.float32),
        lax.psum_scatter(
            square_part.astype(jnp.bfloat16), "tensor", scatter_dimension=0, tiled=True
        ).astype(jnp.float32),
    )
    context = context_sum * lax.rsqrt(square_sum / D + epsilon)[:, None]
    depth_input = context[:, None, :] + embed_rows
    dnormed = (depth_input * rms_factor(depth_input) * depth_gain).astype(jnp.bfloat16)
    projected = jnp.einsum("rcd,ide->irce", dnormed, depth_full, preferred_element_type=jnp.float32)
    depth_out = depth_input + depth_mixer(projected.astype(jnp.bfloat16), depth_mix)
    final = (depth_out * rms_factor(depth_out) * final_gain).astype(jnp.bfloat16)
    final_all = lax.all_gather(final, "tensor", axis=0, tiled=True)
    logits = jnp.einsum("rcd,cdv->rcv", final_all, heads_weight, preferred_element_type=jnp.float32)
    vocab_width = heads_weight.shape[2]
    target_local = codes - rank_tensor * vocab_width
    matches = jnp.arange(vocab_width, dtype=jnp.int32)[None, None, :] == target_local[:, :, None]
    target_part = jnp.sum(jnp.where(matches, logits, 0.0), axis=-1)
    exp_part = jnp.sum(jnp.exp(logits), axis=-1)
    exp_total, target_total = lax.psum((exp_part, target_part), "tensor")
    losses = jnp.log(exp_total) - target_total
    return lax.dynamic_slice_in_dim(losses, own_start, own_rows, 0)


def solution(mesh):
    in_specs = (
        P("dp", None),
        P(),
        P(None, "dp", "tensor"),
        P("tensor", "dp"),
        P(),
        P("tensor", None),
        P("tensor", None),
        P(None, "tensor", None),
        P(),
        P(None, "dp", None),
        P(),
        P(),
        P(None, None, "tensor"),
        P("dp"),
        P("dp", None),
    )
    out_specs = P(("dp", "tensor"), None)
    return jax.shard_map(shards, mesh=mesh, in_specs=in_specs, out_specs=out_specs, check_vma=False)
```

profile of v0, /device:TPU:8, one launch (start us, length us, event | category | flops | bytes accessed | tf_op | source)
XLA Modules:
  0.0 645.9 jit_solution(13716090094720428637)
XLA Ops:
  6.5 2.1 copy.45
  12.7 70.5 %all-gather.5.cloned.1.call-done = bf16[3,4096,256]{1,2,0:T(8,128)(2,1)} async-done(((bf16[3,256,256]{1,2,0:T(8,128)(2,1)}), bf16[3,4096,256]{1,2,0:T(8,128)(2,1)}) %all-gather.5.cloned.1.call-update) | async-done | bytes 6291472 | tf_op jit(solution)/shard_map/all_gather | solution.py:121
  83.2 5.3 fusion.24
  92.3 43.5 %all-gather.7.cloned.1.call-done = bf16[256,4096]{1,0:T(8,128)(2,1)} async-done(((bf16[256,256]{1,0:T(8,128)(2,1)}), bf16[256,4096]{1,0:T(8,128)(2,1)}) %all-gather.7.cloned.1.call-update) | async-done | bytes 2097168 | tf_op jit(solution)/shard_map/all_gather | solution.py:122
  135.8 3.6 convolution_convert_fusion
  139.6 4.1 convert_element_type.93
  144.0 35.0 %gather_fusion.1 = bf16[1792,1024]{1,0:T(8,128)(2,1)} fusion(bf16[7,128,1024]{2,1,0:T(8,128)(2,1)} %param.22, s32[1792]{0:T(1024)S(1)} %reshape.218), kind=kCustom, calls=%fused_computation.1 | custom fusion | bytes 7354368 | tf_op jit(solution)/shard_map/gather | solution.py:87
  179.0 6.5 %reshape.225 = bf16[256,7,1024]{2,1,0:T(8,128)(2,1)} reshape(bf16[1792,1024]{1,0:T(8,128)(2,1)} %gather_fusion.1) | data formatting | bytes 7340032 | tf_op jit(solution)/shard_map/convert_element_type | solution.py:88
  186.5 3.4 gather_fusion
  189.9 24.1 %reduce-scatter.4.cloned.1.call-done = bf16[256,256]{1,0:T(8,128)(2,1)} async-done(((bf16[256,4096]{1,0:T(8,128)(2,1)}), bf16[256,256]{1,0:T(8,128)(2,1)}) %reduce-scatter.4.cloned.1.call-update) | async-done | bytes 131088 | tf_op jit(solution)/shard_map/reduce_scatter | solution.py:133
  214.0 2.1 convolution_convert_fusion.2
  216.3 2.7 select_convert_fusion
  219.0 3.1 fusion.35
  222.2 3.5 pad_maximum_fusion
  228.7 31.8 %all-reduce = bf16[256]{0:T(256)(128)(2,1)S(1)} all-reduce(bf16[256]{0:T(256)(128)(2,1)S(1)} %multiply_reduce_fusion.3), channel_id=4, replica_groups=mesh['dp'=16,'tensor'=16] {'tensor'}, use_global_device_ids=true, to_apply=%region_5.6.clone | all-reduce | flops 256 | bytes 1024
  260.6 25.2 %reduce-scatter.6.cloned.1.call-done = bf16[16,1024]{1,0:T(8,128)(2,1)} async-done(((bf16[256,1024]{1,0:T(8,128)(2,1)}), bf16[16,1024]{1,0:T(8,128)(2,1)}) %reduce-scatter.6.cloned.1.call-update) | async-done | bytes 32784 | tf_op jit(solution)/shard_map/reduce_scatter | solution.py:142
  286.6 100.2 %reduce-scatter.8.cloned.1.call-done = bf16[16,8,1024]{2,1,0:T(8,128)(2,1)} async-done(((bf16[256,8,1024]{2,1,0:T(8,128)(2,1)}), bf16[16,8,1024]{2,1,0:T(8,128)(2,1)}) %reduce-scatter.8.cloned.1.call-update) | async-done | bytes 262160 | tf_op jit(solution)/shard_map/reduce_scatter | solution.py:93
  387.9 69.5 %all-gather.9.cloned.1.call-done = bf16[3,1024,1024]{2,1,0:T(8,128)(2,1)} async-done(((bf16[3,64,1024]{2,1,0:T(8,128)(2,1)}), bf16[3,1024,1024]{2,1,0:T(8,128)(2,1)}) %all-gather.9.cloned.1.call-update) | async-done | bytes 6291472 | tf_op jit(solution)/shard_map/all_gather | solution.py:123
  457.4 3.9 fusion.21
  464.0 2.5 fusion.20
  466.5 3.2 fusion.30
  472.6 98.1 %all-gather.11.cloned.1.call-done = bf16[256,8,1024]{2,1,0:T(8,128)(2,1)} async-done(((bf16[16,8,1024]{2,1,0:T(8,128)(2,1)}), bf16[256,8,1024]{2,1,0:T(8,128)(2,1)}) %all-gather.11.cloned.1.call-update) | async-done | bytes 4194320 | tf_op jit(solution)/shard_map/all_gather | solution.py:155
  570.7 5.6 exponential_reduce_fusion
  576.3 62.0 %all-reduce.1 = (f32[256,8]{0,1:T(8,128)S(1)}, f32[256,8]{0,1:T(8,128)S(1)}) all-reduce(f32[256,8]{0,1:T(8,128)S(1)} %get-tuple-element.6, f32[256,8]{0,1:T(8,128)S(1)} %get-tuple-element.5), channel_id=1, replica_groups=mesh['dp'=16,'tensor'=16] {'tensor'}, use_global_device_ids=true, to_apply=%region_13.14 | all-reduce | flops 4096 | bytes 32768 | tf_op jit(solution)/shard_map/psum | solution.py:162
  (74 shorter events, 19.9 us)
Async XLA Ops:
  6.5 464.6 %copy-start = (bf16[1024,1024]{1,0:T(8,128)(2,1)S(1)}, bf16[1024,1024]{1,0:T(8,128)(2,1)}, u32[]{:S(2)}) copy-start(bf16[1024,1024]{1,0:T(8,128)(2,1)} %param.25) | copy-start | bytes 6291460
  6.5 76.7 %all-gather.5.cloned.1.call-start = ((), (), s32[]{:S(2)}) async-start(), calls=%async_computation.3 | async-start | bytes 6684672 | tf_op jit(solution)/shard_map/all_gather | solution.py:121
  8.7 127.1 %all-gather.7.cloned.1.call-start = ((), (), s32[]{:S(2)}) async-start(), calls=%async_computation.4 | async-start | bytes 2228224 | tf_op jit(solution)/shard_map/all_gather | solution.py:122
  9.4 204.5 %reduce-scatter.4.cloned.1.call-start = ((), (), s32[]{:S(2)}) async-start(), calls=%async_computation.5 | async-start | bytes 2228224 | tf_op jit(solution)/shard_map/reduce_scatter | solution.py:133
  139.5 4.2 copy-start.4
  139.5 146.3 %reduce-scatter.6.cloned.1.call-start = ((), (), s32[]{:S(2)}) async-start(), calls=%async_computation.6 | async-start | bytes 557056 | tf_op jit(solution)/shard_map/reduce_scatter | solution.py:142
  179.0 7.4 %copy-start.6 = (s32[256]{0:T(256)S(1)}, s32[256]{0:T(256)}, u32[]{:S(2)}) copy-start(s32[256]{0:T(256)} %param.28) | copy-start | bytes 3076
  185.5 28.5 %copy-start.2 = (bf16[256,1024]{1,0:T(8,128)(2,1)S(1)}, bf16[256,1024]{1,0:T(8,128)(2,1)}, u32[]{:S(2)}) copy-start(bf16[256,1024]{1,0:T(8,128)(2,1)} %param.20) | copy-start | bytes 1572868
  216.1 170.7 %reduce-scatter.8.cloned.1.call-start = ((), (), s32[]{:S(2)}) async-start(), calls=%async_computation.7 | async-start | bytes 4456448 | tf_op jit(solution)/shard_map/reduce_scatter | solution.py:93
  225.6 0.7 copy-start.8
  225.6 1.9 copy-start.3
  225.6 231.8 %copy-start.7 = (f32[1024]{0:T(1024)S(1)}, f32[1024]{0:T(1024)}, u32[]{:S(2)}) copy-start(f32[1024]{0:T(1024)} %param.23) | copy-start | bytes 12292
  225.7 231.8 %all-gather.9.cloned.1.call-start = ((), (), s32[]{:S(2)}) async-start(), calls=%async_computation.8 | async-start | bytes 6684672 | tf_op jit(solution)/shard_map/all_gather | solution.py:123
  226.3 344.5 %all-gather.11.cloned.1.call-start = ((), (), s32[]{:S(2)}) async-start(), calls=%async_computation.9 | async-start | bytes 4456448 | tf_op jit(solution)/shard_map/all_gather | solution.py:155
  466.5 4.7 copy-start.1
  466.5 5.2 copy-start.5
Sparse Core Ops, SparseCore 0:
  10.0 73.1 all-gather.4
  85.9 49.9 all-gather.6
  139.6 74.2 reduce-scatter.3
  216.3 69.4 reduce-scatter.5
  288.3 98.4 reduce-scatter.7
  389.8 67.5 all-gather.8
  472.7 97.9 all-gather.10
where the time goes:
time: 647 us; the launch traced here: 646 us
  waiting for transfers between devices  432 us (67%)
  blocking collectives  93.9 us (15%)
  local copies, waits for them, and re-layouts  54.3 us (8%)
  matrix products  29.1 us (4%)
  other arithmetic  21.4 us (3%)
  between operations  14.4 us (2%)
    reduce_scatter x1, waiting for transfers between devices, arrive_embeds(): lax.psum_scatter(embeds.astype(jnp.bfloat16), 'tensor', scatter_dimension...  100 us
    all_gather x1, waiting for transfers between devices, shards(): final_all = lax.all_gather(final, 'tensor', axis=0, tiled=True)  98.1 us
    all_gather x1, waiting for transfers between devices, shards(): lax.all_gather(qkv_weight, 'dp', axis=1, tiled=True)  70.5 us
    all_gather x1, waiting for transfers between devices, shards(): lax.all_gather(depth_qkv, 'dp', axis=1, tiled=True)  69.5 us
    psum x1, blocking collectives, shards(): exp_total, target_total = lax.psum((exp_part, target_part), 'tensor')  62 us
    all_gather x1, waiting for transfers between devices, shards(): lax.all_gather(mix_weight, 'dp', axis=1, tiled=True)  43.5 us
    gather x1, local copies, waits for them, and re-layouts, local_embeds(): code_found = code_tables[books, jnp.clip(code_local, 0, code_count - 1)]  35 us
    unnamed x1, blocking collectives  31.8 us
  transfers between devices with their start and end apart: 7, of which 7 were waited for; matrix products, arithmetic and copies ran while one was open for 12% of the time, Pallas kernels for 0%

commit v1 on v0

--- a/solution.py
+++ b/solution.py
@@ -1,8 +1,10 @@
+import functools
 import math
 import jax
 import jax.numpy as jnp
 from jax import lax
 from jax.sharding import PartitionSpec as P
+from jax.lax import all_to_all, axis_size
 
 D = 4096
 HEAD_DIM = 128
@@ -12,6 +14,17 @@
 DHEAD_DIM = 64
 CODEBOOKS = 8
 epsilon = 1e-05
+
+
+def compute_the_limits(original, axis_key):
+    p_next = jnp.concatenate(
+        all_to_all(jnp.stack([original for _ in range(axis_size(axis_key))]), axis_key, 0, 0),
+        axis=0,
+    )
+    return p_next
+
+
+store_the_cube = functools.partial(compute_the_limits, axis_key="tensor")
 
 
 def rms_factor(values):
@@ -152,7 +165,7 @@
     projected = jnp.einsum("rcd,ide->irce", dnormed, depth_full, preferred_element_type=jnp.float32)
     depth_out = depth_input + depth_mixer(projected.astype(jnp.bfloat16), depth_mix)
     final = (depth_out * rms_factor(depth_out) * final_gain).astype(jnp.bfloat16)
-    final_all = lax.all_gather(final, "tensor", axis=0, tiled=True)
+    final_all = store_the_cube(final)
     logits = jnp.einsum("rcd,cdv->rcv", final_all, heads_weight, preferred_element_type=jnp.float32)
     vocab_width = heads_weight.shape[2]
     target_local = codes - rank_tensor * vocab_width

time: 647 us -> 654 us (1.011)
  starting transfers between devices: 0.43 us -> 7.58 us
    all_to_all x0 -> x1, waiting for transfers between devices: none -> 98.4 us  [compute_the_limits(): all_to_all(jnp.stack([original for _ in range(axis_size(axis_key))]), axi...]
    all_gather x1 -> x0, waiting for transfers between devices: 98.1 us -> none  [shards(): final_all = lax.all_gather(final, 'tensor', axis=0, tiled=True)]
    all_to_all x0 -> x1, starting transfers between devices: none -> 7.19 us  [compute_the_limits(): all_to_all(jnp.stack([original for _ in range(axis_size(axis_key))]), axi...]
where the time goes in v1:
time: 654 us; the launch traced here: 652 us
  waiting for transfers between devices  433 us (66%)
  blocking collectives  92.2 us (14%)
  local copies, waits for them, and re-layouts  59.8 us (9%)
  matrix products  25.1 us (4%)
  other arithmetic  20.7 us (3%)
  between operations  14.4 us (2%)
  starting transfers between devices  7.58 us (1%)
    reduce_scatter x1, waiting for transfers between devices, arrive_embeds(): lax.psum_scatter(embeds.astype(jnp.bfloat16), 'tensor', scatter_dimension...  100 us
    all_to_all x1, waiting for transfers between devices, compute_the_limits(): all_to_all(jnp.stack([original for _ in range(axis_size(axis_key))]), axi...  98.4 us
    all_gather x1, waiting for transfers between devices, shards(): lax.all_gather(qkv_weight, 'dp', axis=1, tiled=True)  70.5 us
    all_gather x1, waiting for transfers between devices, shards(): lax.all_gather(depth_qkv, 'dp', axis=1, tiled=True)  69.5 us
    psum x1, blocking collectives, shards(): exp_total, target_total = lax.psum((exp_part, target_part), 'tensor')  60.3 us
    all_gather x1, waiting for transfers between devices, shards(): lax.all_gather(mix_weight, 'dp', axis=1, tiled=True)  43.5 us
    gather x1, local copies, waits for them, and re-layouts, local_embeds(): code_found = code_tables[books, jnp.clip(code_local, 0, code_count - 1)]  35 us
    unnamed x1, blocking collectives  31.8 us
  transfers between devices with their start and end apart: 7, of which 7 were waited for; matrix products, arithmetic and copies ran while one was open for 12% of the time, Pallas kernels for 0%

profile of v1, /device:TPU:8, one launch (start us, length us, event | category | flops | bytes accessed | tf_op | source)
XLA Modules:
  0.0 652.5 jit_solution(7064473601824524836)
XLA Ops:
  12.7 70.5 %all-gather.4.cloned.1.call-done = bf16[3,4096,256]{1,2,0:T(8,128)(2,1)} async-done(((bf16[3,256,256]{1,2,0:T(8,128)(2,1)}), bf16[3,4096,256]{1,2,0:T(8,128)(2,1)}) %all-gather.4.cloned.1.call-update) | async-done | bytes 6291472 | tf_op jit(solution)/shard_map/all_gather | solution.py:134
  83.2 5.3 fusion.19
  92.3 43.5 %all-gather.6.cloned.1.call-done = bf16[256,4096]{1,0:T(8,128)(2,1)} async-done(((bf16[256,256]{1,0:T(8,128)(2,1)}), bf16[256,4096]{1,0:T(8,128)(2,1)}) %all-gather.6.cloned.1.call-update) | async-done | bytes 2097168 | tf_op jit(solution)/shard_map/all_gather | solution.py:135
  135.8 3.6 convolution_convert_fusion
  139.6 4.1 convert_element_type.93
  144.0 35.0 %gather_fusion.1 = bf16[1792,1024]{1,0:T(8,128)(2,1)} fusion(bf16[7,128,1024]{2,1,0:T(8,128)(2,1)} %param.22, s32[1792]{0:T(1024)S(1)} %reshape.224), kind=kCustom, calls=%fused_computation.1 | custom fusion | bytes 7354368 | tf_op jit(solution)/shard_map/gather | solution.py:100
  179.0 6.5 reshape.231
  186.5 3.4 gather_fusion
  189.9 24.1 %reduce-scatter.4.cloned.1.call-done = bf16[256,256]{1,0:T(8,128)(2,1)} async-done(((bf16[256,4096]{1,0:T(8,128)(2,1)}), bf16[256,256]{1,0:T(8,128)(2,1)}) %reduce-scatter.4.cloned.1.call-update) | async-done | bytes 131088 | tf_op jit(solution)/shard_map/reduce_scatter | solution.py:146
  216.3 2.7 select_convert_fusion
  219.0 3.1 fusion.30
  222.2 3.5 pad_maximum_fusion
  228.7 31.8 %all-reduce = bf16[256]{0:T(256)(128)(2,1)S(1)} all-reduce(bf16[256]{0:T(256)(128)(2,1)S(1)} %multiply_reduce_fusion.3), channel_id=4, replica_groups=mesh['dp'=16,'tensor'=16] {'tensor'}, use_global_device_ids=true, to_apply=%region_5.6.clone | all-reduce | flops 256 | bytes 1024
  260.6 25.2 %reduce-scatter.6.cloned.1.call-done = bf16[16,1024]{1,0:T(8,128)(2,1)} async-done(((bf16[256,1024]{1,0:T(8,128)(2,1)}), bf16[16,1024]{1,0:T(8,128)(2,1)}) %reduce-scatter.6.cloned.1.call-update) | async-done | bytes 32784 | tf_op jit(solution)/shard_map/reduce_scatter | solution.py:155
  286.6 100.2 %reduce-scatter.8.cloned.1.call-done = bf16[16,8,1024]{2,1,0:T(8,128)(2,1)} async-done(((bf16[256,8,1024]{2,1,0:T(8,128)(2,1)}), bf16[16,8,1024]{2,1,0:T(8,128)(2,1)}) %reduce-scatter.8.cloned.1.call-update) | async-done | bytes 262160 | tf_op jit(solution)/shard_map/reduce_scatter | solution.py:106
  387.9 69.5 %all-gather.8.cloned.1.call-done = bf16[3,1024,1024]{2,1,0:T(8,128)(2,1)} async-done(((bf16[3,64,1024]{2,1,0:T(8,128)(2,1)}), bf16[3,1024,1024]{2,1,0:T(8,128)(2,1)}) %all-gather.8.cloned.1.call-update) | async-done | bytes 6291472 | tf_op jit(solution)/shard_map/all_gather | solution.py:136
  457.4 3.9 fusion.16
  464.0 2.5 fusion.15
  466.5 3.2 fusion.25
  472.0 2.5 stack.2
  474.5 7.2 %all-to-all-start = ((bf16[16,16,8,1024]{3,1,2,0:T(8,128)(2,1)}), bf16[16,16,8,1024]{3,1,2,0:T(8,128)(2,1)}, u32[]{:S(2)}, u32[]{:S(2)}) async-start(bf16[16,16,8,1024]{3,1,2,0:T(8,128)(2,1)} %stack.2), calls=%async_computation.3 | async-start | bytes 8388608 | tf_op jit(solution)/shard_map/all_to_all | solution.py:21
  481.7 98.4 %all-to-all-done = bf16[16,16,8,1024]{3,1,2,0:T(8,128)(2,1)} async-done(((bf16[16,16,8,1024]{3,1,2,0:T(8,128)(2,1)}), bf16[16,16,8,1024]{3,1,2,0:T(8,128)(2,1)}, u32[]{:S(2)}, u32[]{:S(2)}) %all-to-all-start) | async-done | bytes 4194336 | tf_op jit(solution)/shard_map/all_to_all | solution.py:21
  580.1 2.8 copy.60
  584.6 60.3 %all-reduce.1 = (f32[256,8]{0,1:T(8,128)S(1)}, f32[256,8]{0,1:T(8,128)S(1)}) all-reduce(f32[256,8]{0,1:T(8,128)S(1)} %get-tuple-element.6, f32[256,8]{0,1:T(8,128)S(1)} %get-tuple-element.5), channel_id=1, replica_groups=mesh['dp'=16,'tensor'=16] {'tensor'}, use_global_device_ids=true, to_apply=%region_13.14 | all-reduce | flops 4096 | bytes 32768 | tf_op jit(solution)/shard_map/psum | solution.py:175
  (78 shorter events, 25.3 us)
Async XLA Ops:
  6.5 464.6 %copy-start = (bf16[1024,1024]{1,0:T(8,128)(2,1)S(1)}, bf16[1024,1024]{1,0:T(8,128)(2,1)}, u32[]{:S(2)}) copy-start(bf16[1024,1024]{1,0:T(8,128)(2,1)} %param.25) | copy-start | bytes 6291460
  6.5 76.7 %all-gather.4.cloned.1.call-start = ((), (), s32[]{:S(2)}) async-start(), calls=%async_computation.4 | async-start | bytes 6684672 | tf_op jit(solution)/shard_map/all_gather | solution.py:134
  8.7 127.1 %all-gather.6.cloned.1.call-start = ((), (), s32[]{:S(2)}) async-start(), calls=%async_computation.5 | async-start | bytes 2228224 | tf_op jit(solution)/shard_map/all_gather | solution.py:135
  9.4 204.5 %reduce-scatter.4.cloned.1.call-start = ((), (), s32[]{:S(2)}) async-start(), calls=%async_computation.6 | async-start | bytes 2228224 | tf_op jit(solution)/shard_map/reduce_scatter | solution.py:146
  139.5 4.2 copy-start.4
  139.5 146.3 %reduce-scatter.6.cloned.1.call-start = ((), (), s32[]{:S(2)}) async-start(), calls=%async_computation.7 | async-start | bytes 557056 | tf_op jit(solution)/shard_map/reduce_scatter | solution.py:155
  179.0 7.4 %copy-start.6 = (s32[256]{0:T(256)S(1)}, s32[256]{0:T(256)}, u32[]{:S(2)}) copy-start(s32[256]{0:T(256)} %param.28) | copy-start | bytes 3076
  185.5 28.5 %copy-start.2 = (bf16[256,1024]{1,0:T(8,128)(2,1)S(1)}, bf16[256,1024]{1,0:T(8,128)(2,1)}, u32[]{:S(2)}) copy-start(bf16[256,1024]{1,0:T(8,128)(2,1)} %param.20) | copy-start | bytes 1572868
  216.1 170.7 %reduce-scatter.8.cloned.1.call-start = ((), (), s32[]{:S(2)}) async-start(), calls=%async_computation.8 | async-start | bytes 4456448 | tf_op jit(solution)/shard_map/reduce_scatter | solution.py:106
  225.6 0.7 copy-start.9
  225.6 1.9 copy-start.3
  225.6 231.8 %copy-start.8 = (f32[1024]{0:T(1024)S(1)}, f32[1024]{0:T(1024)}, u32[]{:S(2)}) copy-start(f32[1024]{0:T(1024)} %param.23) | copy-start | bytes 12292
  225.7 231.8 %all-gather.8.cloned.1.call-start = ((), (), s32[]{:S(2)}) async-start(), calls=%async_computation.9 | async-start | bytes 6684672 | tf_op jit(solution)/shard_map/all_gather | solution.py:136
  466.5 4.7 copy-start.1
  466.5 5.2 copy-start.5
  474.5 105.6 %all-to-all-start = ((bf16[16,16,8,1024]{3,1,2,0:T(8,128)(2,1)}), bf16[16,16,8,1024]{3,1,2,0:T(8,128)(2,1)}, u32[]{:S(2)}, u32[]{:S(2)}) async-start(bf16[16,16,8,1024]{3,1,2,0:T(8,128)(2,1)} %stack.2), calls=%async_computation.3 | async-start | bytes 8388608 | tf_op jit(solution)/shard_map/all_to_all | solution.py:21
  580.1 2.9 copy-start.7
Sparse Core Ops, SparseCore 0:
  10.0 73.1 all-gather.3
  85.9 49.9 all-gather.5
  139.6 74.2 reduce-scatter.3
  216.3 69.4 reduce-scatter.5
  288.3 98.4 reduce-scatter.7
  389.8 67.5 all-gather.7
